TPU v7x, 512 devices: a whole 4x8x8 slice. The times are simulated.
512 devices in a mesh: dp: 32 (over y_hi, x, core), seq: 16 (over z, y_lo).
Axes of the slice: x: 4, y: 8 (y_hi: 4, y_lo: 2; y = y_hi * 2 + y_lo), z: 8, core: 2. Of those that a mesh axis runs over, the one named last changes fastest.
Arguments:
- query_rows: bfloat16 [32, 2048, 2048], P('dp', 'seq'), may hold values from -108 to 108
- key_rows: bfloat16 [32, 2048, 2048], P('dp', 'seq'), may hold values from -6 to 6
- value_rows: bfloat16 [32, 2048, 2048], P('dp', 'seq'), may hold values from -6 to 6
- out_weight: bfloat16 [2048, 2048], P('seq', 'dp'), may hold values from -0.125 to 0.125
- grad_out: bfloat16 [32, 2048, 2048], P('dp', 'seq'), may hold values from -6 to 6
- block_list: int32 [32, 32, 8], P('dp'), may hold values from 0 to 31, as said below
Outputs:
- attended: bfloat16 [32, 2048, 2048], P('dp', 'seq')
- query_gradient: bfloat16 [32, 2048, 2048], P('dp', 'seq')
- grad_key: bfloat16 [32, 2048, 2048], P('dp', 'seq')
- grad_value: bfloat16 [32, 2048, 2048], P('dp', 'seq')
- grad_weight: float32 [2048, 2048], P('seq', 'dp')
Inputs may be any that keep to these rules, and one draw needn't show every extreme that they name: `block_list`: for query block b, slots 0 to 2 hold b - 1, b, b + 1 modulo 32, slots 3 and 4 hold 0 and 31, slots 5 to 7 are drawn at random; the same list serves all heads.
All inputs are finite; a program needn't handle non-finite values.
Results may differ from a plain program's by a relative error of at most 0.0075.
Values may be sent and summed in bfloat16 or wider, within the bound.
A program may use at most 128 MiB of HBM per device.

v0:
```python
import math
import jax
import jax.numpy as jnp
from jax import lax
from jax.sharding import PartitionSpec as P

HEAD_SIZE = 128


def spread_weight(weight_sum):
    return lax.psum_scatter(weight_sum, "dp", scatter_dimension=1, tiled=True)


def local(query_rows, key_rows, value_rows, out_weight, grad_out, block_list):
    query_all, key_all, value_all = (
        lax.all_to_all(query_rows, "seq", split_axis=2, concat_axis=1, tiled=True),
        lax.all_to_all(key_rows, "seq", split_axis=2, concat_axis=1, tiled=True),
        lax.all_to_all(value_rows, "seq", split_axis=2, concat_axis=1, tiled=True),
    )
    length = query_all.shape[1]
    width_here = query_all.shape[2]
    heads_here = width_here // HEAD_SIZE
    block_ids = block_list[0]
    block_count = block_ids.shape[0]
    slot_count = block_ids.shape[1]
    block_size = length // block_count
    logit_scale = 1.0 / math.sqrt(HEAD_SIZE)

    def to_heads(flat):
        split = flat.reshape(length, heads_here, HEAD_SIZE).transpose(1, 0, 2)
        return split.reshape(heads_here, block_count, block_size, HEAD_SIZE)

    def to_flat(blocked):
        joined = blocked.reshape(heads_here, length, HEAD_SIZE).transpose(1, 0, 2)
        return joined.reshape(1, length, width_here)

    blocked_queries = to_heads(query_all[0])
    key_block_indices = to_heads(key_all[0])[:, block_ids].reshape(
        heads_here, block_count, slot_count * block_size, HEAD_SIZE
    )
    value_block_indices = to_heads(value_all[0])[:, block_ids].reshape(
        heads_here, block_count, slot_count * block_size, HEAD_SIZE
    )
    attention_logits = (
        jnp.einsum(
            "hbqd,hbkd->hbqk",
            blocked_queries,
            key_block_indices,
            preferred_element_type=jnp.float32,
        )
        * logit_scale
    )
    highest = jnp.max(attention_logits, axis=-1, keepdims=True)
    expo = jnp.exp(attention_logits - highest)
    attn_probs = expo / jnp.sum(expo, axis=-1, keepdims=True)
    reduced_probabilities = attn_probs.astype(jnp.bfloat16)
    attended = jnp.einsum(
        "hbqk,hbkd->hbqd",
        reduced_probabilities,
        value_block_indices,
        preferred_element_type=jnp.float32,
    ).astype(jnp.bfloat16)
    attended_flat = to_flat(attended)
    attended_seq = lax.all_to_all(attended_flat, "seq", split_axis=1, concat_axis=2, tiled=True)
    weight_here = lax.all_gather(out_weight, "dp", axis=1, tiled=True)
    gathered_grad = lax.all_gather(grad_out, "seq", axis=1, tiled=True)[0]
    grad_flat = lax.dot_general(
        gathered_grad, weight_here, (((1,), (1,)), ((), ())), preferred_element_type=jnp.float32
    ).astype(jnp.bfloat16)
    weight_sum = lax.dot_general(
        attended_flat[0],
        gathered_grad,
        (((0,), (0,)), ((), ())),
        preferred_element_type=jnp.float32,
    )
    weight_part = None
    gradient_per_block = to_heads(grad_flat)
    value_contributions = jnp.einsum(
        "hbqk,hbqd->hbkd",
        reduced_probabilities,
        gradient_per_block,
        preferred_element_type=jnp.float32,
    )
    probability_gradient = jnp.einsum(
        "hbqd,hbkd->hbqk",
        gradient_per_block,
        value_block_indices,
        preferred_element_type=jnp.float32,
    )
    row_delta = jnp.sum(attn_probs * probability_gradient, axis=-1, keepdims=True)
    score_gradient = (attn_probs * (probability_gradient - row_delta) * logit_scale).astype(
        jnp.bfloat16
    )
    query_gradient = jnp.einsum(
        "hbqk,hbkd->hbqd", score_gradient, key_block_indices, preferred_element_type=jnp.float32
    ).astype(jnp.bfloat16)
    key_contributions = jnp.einsum(
        "hbqk,hbqd->hbkd", score_gradient, blocked_queries, preferred_element_type=jnp.float32
    )
    one_hot = (
        block_ids[:, :, None] == jnp.arange(block_count, dtype=jnp.int32)[None, None, :]
    ).astype(jnp.float32)

    def collect(terms):
        spread = terms.reshape(heads_here, block_count, slot_count, block_size * HEAD_SIZE)
        summed = jnp.einsum(
            "hqsx,qsk->hkx",
            spread,
            one_hot,
            precision=lax.Precision.HIGHEST,
            preferred_element_type=jnp.float32,
        )
        return summed.reshape(heads_here, block_count, block_size, HEAD_SIZE).astype(jnp.bfloat16)

    grad_key = collect(key_contributions)
    grad_value = collect(value_contributions)
    weight_part = spread_weight(weight_sum)
    query_back, key_back, value_back = (
        lax.all_to_all(to_flat(query_gradient), "seq", split_axis=1, concat_axis=2, tiled=True),
        lax.all_to_all(to_flat(grad_key), "seq", split_axis=1, concat_axis=2, tiled=True),
        lax.all_to_all(to_flat(grad_value), "seq", split_axis=1, concat_axis=2, tiled=True),
    )
    return (attended_seq, query_back, key_back, value_back, weight_part)


def solution(mesh):
    return jax.shard_map(
        local,
        mesh=mesh,
        in_specs=(
            P("dp", "seq", None),
            P("dp", "seq", None),
            P("dp", "seq", None),
            P("seq", "dp"),
            P("dp", "seq", None),
            P("dp", None, None),
        ),
        out_specs=(
            P("dp", "seq", None),
            P("dp", "seq", None),
            P("dp", "seq", None),
            P("dp", "seq", None),
            P("seq", "dp"),
        ),
        check_vma=False,
    )
```

profile of v0, /device:TPU:22, one launch (start us, length us, event | category | flops | bytes accessed | tf_op | source)
XLA Modules:
  0.0 454.0 jit_solution(4954409773281861823)
XLA Ops:
  7.2 0.7 all-gather.2.cloned.1.call-update
  7.9 2.4 copy.81
  10.3 0.5 broadcast.67
  10.8 11.6 %reduce.8 = bf16[2048,128]{1,0:T(8,128)(2,1)S(1)} reduce(bf16[2048,1,128]{2,1,0:T(2,128)(2,1)S(1)} %bitcast.142, bf16[]{:T(256)} %broadcast.67), dimensions={1}, to_apply=%bitcast.91.reduce_sub_computation | reduce | bytes 1048578
  22.4 0.9 reshape.177
  23.3 11.4 %all-to-all-start.1 = ((bf16[16,2,8192]{2,1,0:T(2,128)(2,1)}), bf16[16,2,8192]{2,1,0:T(2,128)(2,1)S(1)}, u32[]{:S(2)}, u32[]{:S(2)}) async-start(bf16[16,2,8192]{2,1,0:T(2,128)(2,1)} %reshape.177), calls=%async_computation.1 | async-start | bytes 1048576 | tf_op jit(solution)/shard_map/all_to_all | solution.py:16
  34.7 0.8 copy.78
  35.5 11.5 %reduce.7 = bf16[2048,128]{1,0:T(8,128)(2,1)S(1)} reduce(bf16[2048,1,128]{2,1,0:T(2,128)(2,1)S(1)} %bitcast.146, bf16[]{:T(256)} %broadcast.67), dimensions={1}, to_apply=%bitcast.89.reduce_sub_computation | reduce | bytes 1048578
  47.1 0.9 reshape.175
  48.0 8.3 %all-to-all-done.1 = bf16[16,2,8192]{2,1,0:T(2,128)(2,1)S(1)} async-done(((bf16[16,2,8192]{2,1,0:T(2,128)(2,1)}), bf16[16,2,8192]{2,1,0:T(2,128)(2,1)S(1)}, u32[]{:S(2)}, u32[]{:S(2)}) %all-to-all-start.1) | async-done | bytes 524320 | tf_op jit(solution)/shard_map/all_to_all | solution.py:16
  56.3 14.0 %all-to-all-start = ((bf16[16,2,8192]{2,1,0:T(2,128)(2,1)}), bf16[16,2,8192]{2,1,0:T(2,128)(2,1)S(1)}, u32[]{:S(2)}, u32[]{:S(2)}) async-start(bf16[16,2,8192]{2,1,0:T(2,128)(2,1)} %reshape.175), calls=%async_computation | async-start | bytes 1048576 | tf_op jit(solution)/shard_map/all_to_all | solution.py:17
  70.3 0.8 copy.83
  71.1 11.5 %reduce.6 = bf16[2048,128]{1,0:T(8,128)(2,1)S(1)} reduce(bf16[2048,1,128]{2,1,0:T(2,128)(2,1)S(1)} %bitcast.147, bf16[]{:T(256)} %broadcast.67), dimensions={1}, to_apply=%bitcast.87.reduce_sub_computation | reduce | bytes 1048578
  82.6 0.9 reshape.173
  83.5 6.8 %all-to-all-done = bf16[16,2,8192]{2,1,0:T(2,128)(2,1)S(1)} async-done(((bf16[16,2,8192]{2,1,0:T(2,128)(2,1)}), bf16[16,2,8192]{2,1,0:T(2,128)(2,1)S(1)}, u32[]{:S(2)}, u32[]{:S(2)}) %all-to-all-start) | async-done | bytes 524320 | tf_op jit(solution)/shard_map/all_to_all | solution.py:17
  90.4 4.0 all-to-all-start.2
  94.6 51.6 %all_gather.7 = bf16[128,2048]{0,1:T(8,128)(2,1)} all-gather(bf16[128,64]{0,1:T(8,128)(2,1)S(1)} %copy-done.7), channel_id=1, replica_groups=mesh['dp'=32,'seq'=16] {'dp'}, dimensions={1}, use_global_device_ids=true | all-gather | bytes 540672 | tf_op jit(solution)/shard_map/all_gather | solution.py:65
  146.3 0.5 reshape.178
  146.9 0.3 copy.82
  147.2 0.5 reshape.176
  147.8 0.3 copy.79
  148.1 0.5 reshape.174
  149.0 3.1 gather_fusion.1
  152.1 3.1 gather_fusion
  155.1 5.8 %fusion.58 = (f32[32,64]{1,0:T(8,128)S(1)}, f32[32,64,512]{2,1,0:T(8,128)}) fusion(bf16[32,512,128]{2,1,0:T(8,128)(2,1)} %bitcast.140, bf16[32,64,128]{2,1,0:T(8,128)(2,1)S(1)} %bitcast.167), kind=kOutput, calls=%fused_computation.49 | convolution fusion | flops 271581696 | bytes 8921088 | tf_op jit(solution)/shard_map/sub | solution.py:54
  161.0 4.4 convolution_convert_fusion
  165.4 8.1 %copy.135 = bf16[1,2048,128]{2,0,1:T(2,128)(2,1)S(1)} copy(bf16[1,2048,128]{2,1,0:T(8,128)(2,1)S(1)} %bitcast.149) | data formatting | bytes 1048576 | tf_op jit(solution)/shard_map/reshape;transpose;reshape | solution.py:35
  173.5 11.9 %reduce.9 = bf16[2048,128]{1,0:T(8,128)(2,1)S(1)} reduce(bf16[2048,1,128]{2,1,0:T(2,128)(2,1)S(1)} %bitcast.148, bf16[]{:T(256)} %broadcast.67), dimensions={1}, to_apply=%bitcast.124.reduce_sub_computation | reduce | bytes 1048578
  185.5 0.9 reshape.179
  186.4 8.3 %all-to-all-start.3 = ((bf16[16,2,8192]{2,1,0:T(2,128)(2,1)}), bf16[16,2,8192]{2,1,0:T(2,128)(2,1)S(1)}, u32[]{:S(2)}, u32[]{:S(2)}) async-start(bf16[16,2,8192]{2,1,0:T(2,128)(2,1)} %reshape.179), calls=%async_computation.3 | async-start | bytes 1048576 | tf_op jit(solution)/shard_map/all_to_all | solution.py:64
  194.7 36.4 %all-gather.2.cloned.1.call-done = bf16[1,2048,2048]{2,1,0:T(8,128)(2,1)} async-done(((bf16[1,128,2048]{2,1,0:T(8,128)(2,1)}), bf16[1,2048,2048]{2,1,0:T(8,128)(2,1)}) %all-gather.2.cloned.1.call-update) | async-done | bytes 8388624 | tf_op jit(solution)/shard_map/all_gather | solution.py:66
  231.1 5.9 %fusion.18 = bf16[2048,128]{1,0:T(8,128)(2,1)S(1)} fusion(bf16[128,2048]{0,1:T(8,128)(2,1)S(1)} %copy-done.5, bf16[1,2048,2048]{2,1,0:T(8,128)(2,1)} %all-gather.2.cloned.1.call-done), kind=kOutput, calls=%fused_computation.22 | convolution fusion | flops 1074003968 | bytes 9437184 | tf_op jit(solution)/shard_map/dot_general | solution.py:67
  237.0 3.5 fusion.61
  240.6 18.6 %fusion.42 = bf16[32,64,128]{2,1,0:T(8,128)(2,1)S(1)} fusion(bf16[32,512,128]{2,1,0:T(8,128)(2,1)} %bitcast.141, f32[32,64,512]{2,1,0:T(8,128)} %fusion.61, f32[32,64,512]{2,1,0:T(8,128)} %get-tuple-element.26, f32[32,64]{1,0:T(8,128)S(1)} %get-tuple-element.25), kind=kOutput, calls=%fused_computation.34 | convolution fusion | flops 276040192 | bytes 13115392 | tf_op jit(solution)/shard_map/hbqk,hbkd->hbqd/dot_general | solution.py:94
  259.2 8.1 %copy.134 = bf16[1,2048,128]{2,0,1:T(2,128)(2,1)S(1)} copy(bf16[1,2048,128]{2,1,0:T(8,128)(2,1)S(1)} %bitcast.166) | data formatting | bytes 1048576 | tf_op jit(solution)/shard_map/reshape;transpose;reshape | solution.py:35
  267.3 11.7 %reduce.10 = bf16[2048,128]{1,0:T(8,128)(2,1)S(1)} reduce(bf16[2048,1,128]{2,1,0:T(2,128)(2,1)S(1)} %bitcast.144, bf16[]{:T(256)} %broadcast.67), dimensions={1}, to_apply=%bitcast.123.reduce_sub_computation | reduce | bytes 1048578
  279.0 0.9 reshape.181
  279.9 8.8 %all-to-all-start.4 = ((bf16[16,2,8192]{2,1,0:T(2,128)(2,1)}), bf16[16,2,8192]{2,1,0:T(2,128)(2,1)S(1)}, u32[]{:S(2)}, u32[]{:S(2)}) async-start(bf16[16,2,8192]{2,1,0:T(2,128)(2,1)} %reshape.181), calls=%async_computation.4 | async-start | bytes 1048576 | tf_op jit(solution)/shard_map/all_to_all | solution.py:119
  288.8 7.8 %fusion.2 = f32[128,2048]{0,1:T(8,128)} fusion(bf16[2048,128]{1,0:T(8,128)(2,1)S(1)} %bitcast.150, bf16[1,2048,2048]{2,1,0:T(8,128)(2,1)} %all-gather.2.cloned.1.call-done), kind=kOutput, calls=%fused_computation.6 | convolution fusion | flops 1073741824 | bytes 9961472 | tf_op jit(solution)/shard_map/dot_general | solution.py:70
  296.6 21.3 %fusion.22 = f32[32,512,128]{2,1,0:T(8,128)} fusion(bf16[32,64,128]{2,1,0:T(8,128)(2,1)S(1)} %bitcast.168, f32[32,64,512]{2,1,0:T(8,128)} %fusion.61, f32[32,64,512]{2,1,0:T(8,128)} %get-tuple-element.26, f32[32,64]{1,0:T(8,128)S(1)} %get-tuple-element.25), kind=kOutput, calls=%fused_computation.23 | convolution fusion | flops 275778048 | bytes 17309696 | tf_op jit(solution)/shard_map/hbqk,hbqd->hbkd/dot_general | solution.py:97
  317.9 9.6 %reshape.140 = f32[32,8,8192]{2,1,0:T(8,128)} reshape(f32[32,512,128]{2,1,0:T(8,128)} %fusion.22) | data formatting | bytes 16777216 | tf_op jit(solution)/shard_map/reshape.33
  327.6 5.1 %copy.131 = f32[32,8,64,128]{3,2,1,0:T(8,128)S(1)} copy(f32[32,8,64,128]{3,1,2,0:T(8,128)} %bitcast.127) | data formatting | bytes 16777216
  332.6 8.2 %fusion.39 = bf16[32,64,128]{2,0,1:T(8,128)(2,1)S(1)} fusion(f32[64,128,32,8]{1,0,3,2:T(8,128)S(1)} %bitcast.128, s32[32,8]{0,1:T(8,128)S(1)} %bitcast.169), kind=kOutput, calls=%fused_computation.32 | convolution fusion | flops 805576704 | bytes 8913920 | tf_op jit(solution)/shard_map/hqsx,qsk->hkx/dot_general | solution.py:106
  341.0 8.5 %copy.133 = bf16[1,2048,128]{2,0,1:T(2,128)(2,1)S(1)} copy(bf16[1,2048,128]{2,1,0:T(8,128)(2,1)S(1)} %bitcast.154) | data formatting | bytes 1048576 | tf_op jit(solution)/shard_map/reshape;transpose;reshape | solution.py:35
  349.6 11.5 %reduce.11 = bf16[2048,128]{1,0:T(8,128)(2,1)S(1)} reduce(bf16[2048,1,128]{2,1,0:T(2,128)(2,1)S(1)} %bitcast.145, bf16[]{:T(256)} %broadcast.67), dimensions={1}, to_apply=%bitcast.122.reduce_sub_computation | reduce | bytes 1048578
  361.1 0.9 reshape.183
  362.0 8.3 %all-to-all-start.5 = ((bf16[16,2,8192]{2,1,0:T(2,128)(2,1)}), bf16[16,2,8192]{2,1,0:T(2,128)(2,1)S(1)}, u32[]{:S(2)}, u32[]{:S(2)}) async-start(bf16[16,2,8192]{2,1,0:T(2,128)(2,1)} %reshape.183), calls=%async_computation.5 | async-start | bytes 1048576 | tf_op jit(solution)/shard_map/all_to_all | solution.py:120
  370.3 7.2 %fusion.45 = f32[32,512,128]{2,1,0:T(8,128)} fusion(bf16[32,64,128]{2,1,0:T(8,128)(2,1)S(1)} %bitcast.165, f32[32,64,512]{2,1,0:T(8,128)} %get-tuple-element.26, f32[32,64]{1,0:T(8,128)S(1)} %get-tuple-element.25), kind=kOutput, calls=%fused_computation.35 | convolution fusion | flops 270532608 | bytes 13115392 | tf_op jit(solution)/shard_map/hbqk,hbqd->hbkd/dot_general | solution.py:78
  377.5 9.4 %reshape.141 = f32[32,8,8192]{2,1,0:T(8,128)} reshape(f32[32,512,128]{2,1,0:T(8,128)} %fusion.45) | data formatting | bytes 16777216 | tf_op jit(solution)/shard_map/reshape.40
  386.9 5.0 %copy.130 = f32[32,8,64,128]{3,2,1,0:T(8,128)S(1)} copy(f32[32,8,64,128]{3,1,2,0:T(8,128)} %bitcast.129) | data formatting | bytes 16777216
  391.9 8.2 %fusion.36 = bf16[32,64,128]{2,0,1:T(8,128)(2,1)S(1)} fusion(f32[64,128,32,8]{1,0,3,2:T(8,128)S(1)} %bitcast.130, s32[32,8]{0,1:T(8,128)S(1)} %bitcast.170), kind=kOutput, calls=%fused_computation.31 | convolution fusion | flops 805576704 | bytes 8913920 | tf_op jit(solution)/shard_map/hqsx,qsk->hkx/dot_general | solution.py:106
  400.3 8.3 %copy.132 = bf16[1,2048,128]{2,0,1:T(2,128)(2,1)S(1)} copy(bf16[1,2048,128]{2,1,0:T(8,128)(2,1)S(1)} %bitcast.155) | data formatting | bytes 1048576 | tf_op jit(solution)/shard_map/reshape;transpose;reshape | solution.py:35
  408.6 11.5 %reduce.12 = bf16[2048,128]{1,0:T(8,128)(2,1)S(1)} reduce(bf16[2048,1,128]{2,1,0:T(2,128)(2,1)S(1)} %bitcast.143, bf16[]{:T(256)} %broadcast.67), dimensions={1}, to_apply=%bitcast.121.reduce_sub_computation | reduce | bytes 1048578
  420.2 0.9 reshape.185
  421.1 8.2 %all-to-all-start.6 = ((bf16[16,2,8192]{2,1,0:T(2,128)(2,1)}), bf16[16,2,8192]{2,1,0:T(2,128)(2,1)S(1)}, u32[]{:S(2)}, u32[]{:S(2)}) async-start(bf16[16,2,8192]{2,1,0:T(2,128)(2,1)} %reshape.185), calls=%async_computation.6 | async-start | bytes 1048576 | tf_op jit(solution)/shard_map/all_to_all | solution.py:121
  429.3 0.5 reshape.180
  430.2 1.0 copy.97
  431.2 0.5 reshape.182
  432.1 1.0 copy.98
  433.1 0.5 reshape.184
  434.0 1.0 copy.99
  435.0 10.0 %all-to-all-done.6 = bf16[16,2,8192]{2,1,0:T(2,128)(2,1)S(1)} async-done(((bf16[16,2,8192]{2,1,0:T(2,128)(2,1)}), bf16[16,2,8192]{2,1,0:T(2,128)(2,1)S(1)}, u32[]{:S(2)}, u32[]{:S(2)}) %all-to-all-start.6) | async-done | bytes 524320 | tf_op jit(solution)/shard_map/all_to_all | solution.py:121
  445.1 0.5 reshape.186
  445.9 1.0 copy.100
  (42 shorter events, 2.6 us)
Async XLA Ops:
  7.2 27.6 %copy-start.1 = (bf16[1,128,2048]{2,1,0:T(8,128)(2,1)S(1)}, bf16[1,128,2048]{2,1,0:T(8,128)(2,1)}, u32[]{:S(2)}) copy-start(bf16[1,128,2048]{2,1,0:T(8,128)(2,1)} %param.7) | copy-start | bytes 1572868
  7.2 224.0 %all-gather.2.cloned.1.call-start = ((), (), s32[]{:S(2)}) async-start(), calls=%async_computation.8 | async-start | bytes 8912896 | tf_op jit(solution)/shard_map/all_gather | solution.py:66
  10.8 59.5 %copy-start.2 = (bf16[1,128,2048]{2,1,0:T(8,128)(2,1)S(1)}, bf16[1,128,2048]{2,1,0:T(8,128)(2,1)}, u32[]{:S(2)}) copy-start(bf16[1,128,2048]{2,1,0:T(8,128)(2,1)} %param.8) | copy-start | bytes 1572868
  23.3 33.0 %all-to-all-start.1 = ((bf16[16,2,8192]{2,1,0:T(2,128)(2,1)}), bf16[16,2,8192]{2,1,0:T(2,128)(2,1)S(1)}, u32[]{:S(2)}, u32[]{:S(2)}) async-start(bf16[16,2,8192]{2,1,0:T(2,128)(2,1)} %reshape.177), calls=%async_computation.1 | async-start | bytes 1048576 | tf_op jit(solution)/shard_map/all_to_all | solution.py:16
  35.5 58.9 %copy-start.6 = (s32[1,32,8]{1,2,0:T(8,128)S(1)}, s32[1,32,8]{1,2,0:T(8,128)}, u32[]{:S(2)}) copy-start(s32[1,32,8]{1,2,0:T(8,128)} %param.11) | copy-start | bytes 3076
  35.5 59.1 %copy-start.7 = (bf16[128,64]{0,1:T(8,128)(2,1)S(1)}, bf16[128,64]{0,1:T(8,128)(2,1)}, u32[]{:S(2)}) copy-start(bf16[128,64]{0,1:T(8,128)(2,1)} %param.9) | copy-start | bytes 49156
  56.3 34.1 %all-to-all-start = ((bf16[16,2,8192]{2,1,0:T(2,128)(2,1)}), bf16[16,2,8192]{2,1,0:T(2,128)(2,1)S(1)}, u32[]{:S(2)}, u32[]{:S(2)}) async-start(bf16[16,2,8192]{2,1,0:T(2,128)(2,1)} %reshape.175), calls=%async_computation | async-start | bytes 1048576 | tf_op jit(solution)/shard_map/all_to_all | solution.py:17
  90.4 57.7 %all-to-all-start.2 = ((bf16[16,2,8192]{2,1,0:T(2,128)(2,1)}), bf16[16,2,8192]{2,1,0:T(2,128)(2,1)S(1)}, u32[]{:S(2)}, u32[]{:S(2)}) async-start(bf16[16,2,8192]{2,1,0:T(2,128)(2,1)} %reshape.173), calls=%async_computation.2 | async-start | bytes 1048576 | tf_op jit(solution)/shard_map/all_to_all | solution.py:18
  147.2 8.0 %copy-start.3 = (bf16[1,16,128,128]{3,2,1,0:T(8,128)(2,1)}, bf16[1,16,128,128]{3,2,1,0:T(8,128)(2,1)S(1)}, u32[]{:S(2)}) copy-start(bf16[1,16,128,128]{3,2,1,0:T(8,128)(2,1)S(1)} %copy.82) | copy-start | bytes 1572868
  165.4 65.8 %copy-start.5 = (bf16[128,2048]{0,1:T(8,128)(2,1)S(1)}, bf16[128,2048]{0,1:T(8,128)(2,1)}, u32[]{:S(2)}) copy-start(bf16[128,2048]{0,1:T(8,128)(2,1)} %all_gather.7) | copy-start | bytes 1572868
  186.4 93.5 %all-to-all-start.3 = ((bf16[16,2,8192]{2,1,0:T(2,128)(2,1)}), bf16[16,2,8192]{2,1,0:T(2,128)(2,1)S(1)}, u32[]{:S(2)}, u32[]{:S(2)}) async-start(bf16[16,2,8192]{2,1,0:T(2,128)(2,1)} %reshape.179), calls=%async_computation.3 | async-start | bytes 1048576 | tf_op jit(solution)/shard_map/all_to_all | solution.py:64
  231.1 5.9 %copy-start = (bf16[256,64,128]{2,1,0:T(8,128)(2,1)S(1)}, bf16[256,64,128]{2,1,0:T(8,128)(2,1)}, u32[]{:S(2)}) copy-start(bf16[256,64,128]{2,1,0:T(8,128)(2,1)} %gather_fusion.1) | copy-start | bytes 12582916
  279.9 82.1 %all-to-all-start.4 = ((bf16[16,2,8192]{2,1,0:T(2,128)(2,1)}), bf16[16,2,8192]{2,1,0:T(2,128)(2,1)S(1)}, u32[]{:S(2)}, u32[]{:S(2)}) async-start(bf16[16,2,8192]{2,1,0:T(2,128)(2,1)} %reshape.181), calls=%async_computation.4 | async-start | bytes 1048576 | tf_op jit(solution)/shard_map/all_to_all | solution.py:119
  288.7 158.2 %reduce-scatter.2.cloned.1.call-start = ((), (), s32[]{:S(2)}) async-start(), calls=%async_computation.9 | async-start | bytes 1081344 | tf_op jit(solution)/shard_map/reduce_scatter | solution.py:11
  288.8 7.8 %copy-start.4 = (bf16[1,16,128,128]{3,2,1,0:T(8,128)(2,1)S(1)}, bf16[1,16,128,128]{3,2,1,0:T(8,128)(2,1)}, u32[]{:S(2)}) copy-start(bf16[1,16,128,128]{3,2,1,0:T(8,128)(2,1)} %copy-done.3) | copy-start | bytes 1572868
  362.0 59.1 %all-to-all-start.5 = ((bf16[16,2,8192]{2,1,0:T(2,128)(2,1)}), bf16[16,2,8192]{2,1,0:T(2,128)(2,1)S(1)}, u32[]{:S(2)}, u32[]{:S(2)}) async-start(bf16[16,2,8192]{2,1,0:T(2,128)(2,1)} %reshape.183), calls=%async_computation.5 | async-start | bytes 1048576 | tf_op jit(solution)/shard_map/all_to_all | solution.py:120
  421.1 24.0 %all-to-all-start.6 = ((bf16[16,2,8192]{2,1,0:T(2,128)(2,1)}), bf16[16,2,8192]{2,1,0:T(2,128)(2,1)S(1)}, u32[]{:S(2)}, u32[]{:S(2)}) async-start(bf16[16,2,8192]{2,1,0:T(2,128)(2,1)} %reshape.185), calls=%async_computation.6 | async-start | bytes 1048576 | tf_op jit(solution)/shard_map/all_to_all | solution.py:121
Sparse Core Ops, SparseCore 0:
  10.1 221.0 all-gather.1
  296.7 95.7 reduce-scatter.1
where the time goes:
time: 463 us; the launch traced here: 454 us
  matrix products  90.8 us (20%)
  local copies, waits for them, and re-layouts  90 us (19%)
  other arithmetic  81.4 us (18%)
  starting transfers between devices  63.2 us (14%)
  waiting for transfers between devices  62.3 us (13%)
  blocking collectives  51.6 us (11%)
  between operations  14.7 us (3%)
    unnamed x7, other arithmetic  81.4 us
    all_gather x1, blocking collectives, local(): weight_here = lax.all_gather(out_weight, 'dp', axis=1, tiled=True)  51.6 us
    all_gather x1, waiting for transfers between devices, local(): gathered_grad = lax.all_gather(grad_out, 'seq', axis=1, tiled=True)[0]  36.4 us
    another operation x4, local copies, waits for them, and re-layouts, to_flat(): return joined.reshape(1, length, width_here)  33.2 us
    unnamed x47, local copies, waits for them, and re-layouts  29.2 us
    dot_general x1, matrix products, local(): jnp.einsum('hbqk,hbqd->hbkd', score_gradient, blocked_queries, preferred_...  21.3 us
    another operation x2, local copies, waits for them, and re-layouts  19 us
    dot_general x1, matrix products, local(): jnp.einsum('hbqk,hbkd->hbqd', score_gradient, key_block_indices, preferre...  18.6 us
  transfers between devices with their start and end apart: 9, of which 4 were waited for; matrix products, arithmetic and copies ran while one was open for 58% of the time, Pallas kernels for 0%

commit v1 on v0

--- a/solution.py
+++ b/solution.py
@@ -1,3 +1,4 @@
+import functools
 import math
 import jax
 import jax.numpy as jnp
@@ -5,6 +6,15 @@
 from jax.sharding import PartitionSpec as P
 
 HEAD_SIZE = 128
+
+
+def _choose_view(t0, row_axis, k_dim):
+    mid_arr = jnp.stack([t0 for _ in range(lax.axis_size(row_axis))])
+    x_next = lax.all_to_all(mid_arr, row_axis, 0, 0)
+    return jnp.concatenate(x_next, axis=k_dim)
+
+
+field_draw = functools.partial(_choose_view, row_axis="dp", k_dim=1)
 
 
 def spread_weight(weight_sum):
@@ -62,7 +72,7 @@
     ).astype(jnp.bfloat16)
     attended_flat = to_flat(attended)
     attended_seq = lax.all_to_all(attended_flat, "seq", split_axis=1, concat_axis=2, tiled=True)
-    weight_here = lax.all_gather(out_weight, "dp", axis=1, tiled=True)
+    weight_here = field_draw(out_weight)
     gathered_grad = lax.all_gather(grad_out, "seq", axis=1, tiled=True)[0]
     grad_flat = lax.dot_general(
         gathered_grad, weight_here, (((1,), (1,)), ((), ())), preferred_element_type=jnp.float32

time: 463 us -> 470 us (1.015)
  the two profiles are of different devices: /device:TPU:22 before, /device:TPU:40 now
where the time goes in v1:
time: 470 us; the launch traced here: 461 us
  waiting for transfers between devices  113 us (24%)
  local copies, waits for them, and re-layouts  90.6 us (19%)
  matrix products  90.2 us (19%)
  other arithmetic  81.5 us (17%)
  starting transfers between devices  70.8 us (15%)
  between operations  14.6 us (3%)
    unnamed x7, other arithmetic  81.5 us
    all_gather x1, waiting for transfers between devices, local(): gathered_grad = lax.all_gather(grad_out, 'seq', axis=1, tiled=True)[0]  80 us
    another operation x4, local copies, waits for them, and re-layouts, to_flat(): return joined.reshape(1, length, width_here)  32.9 us
    unnamed x45, local copies, waits for them, and re-layouts  29.1 us
    dot_general x1, matrix products, local(): jnp.einsum('hbqk,hbqd->hbkd', score_gradient, blocked_queries, preferred_...  20.8 us
    another operation x2, local copies, waits for them, and re-layouts  19 us
    dot_general x1, matrix products, local(): jnp.einsum('hbqk,hbkd->hbqd', score_gradient, key_block_indices, preferre...  18.6 us
    dot_general x2, matrix products, collect(): jnp.einsum('hqsx,qsk->hkx', spread, one_hot, precision=lax.Precision.HIGH...  16.3 us
  transfers between devices with their start and end apart: 10, of which 5 were waited for; matrix products, arithmetic and copies ran while one was open for 57% of the time, Pallas kernels for 0%

profile of v1, /device:TPU:40, one launch (start us, length us, event | category | flops | bytes accessed | tf_op | source)
XLA Modules:
  0.0 460.9 jit_solution(9392119995237609170)
XLA Ops:
  7.2 0.7 all-gather.2.cloned.1.call-update
  7.9 2.4 copy.82
  10.3 0.5 broadcast.69
  10.8 11.6 %reduce.8 = bf16[2048,128]{1,0:T(8,128)(2,1)S(1)} reduce(bf16[2048,1,128]{2,1,0:T(2,128)(2,1)S(1)} %bitcast.145, bf16[]{:T(256)} %broadcast.69), dimensions={1}, to_apply=%bitcast.94.reduce_sub_computation | reduce | bytes 1048578
  22.4 0.9 reshape.187
  23.3 11.8 %all-to-all-start.1 = ((bf16[16,2,8192]{2,1,0:T(2,128)(2,1)}), bf16[16,2,8192]{2,1,0:T(2,128)(2,1)S(1)}, u32[]{:S(2)}, u32[]{:S(2)}) async-start(bf16[16,2,8192]{2,1,0:T(2,128)(2,1)} %reshape.187), calls=%async_computation.1 | async-start | bytes 1048576 | tf_op jit(solution)/shard_map/all_to_all | solution.py:26
  35.1 0.8 copy.79
  35.9 11.5 %reduce.7 = bf16[2048,128]{1,0:T(8,128)(2,1)S(1)} reduce(bf16[2048,1,128]{2,1,0:T(2,128)(2,1)S(1)} %bitcast.149, bf16[]{:T(256)} %broadcast.69), dimensions={1}, to_apply=%bitcast.92.reduce_sub_computation | reduce | bytes 1048578
  47.4 0.9 reshape.185
  48.3 2.8 all-to-all-done.1
  51.1 9.7 %all-to-all-start = ((bf16[16,2,8192]{2,1,0:T(2,128)(2,1)}), bf16[16,2,8192]{2,1,0:T(2,128)(2,1)S(1)}, u32[]{:S(2)}, u32[]{:S(2)}) async-start(bf16[16,2,8192]{2,1,0:T(2,128)(2,1)} %reshape.185), calls=%async_computation | async-start | bytes 1048576 | tf_op jit(solution)/shard_map/all_to_all | solution.py:27
  60.8 0.8 copy.84
  61.6 11.5 %reduce.6 = bf16[2048,128]{1,0:T(8,128)(2,1)S(1)} reduce(bf16[2048,1,128]{2,1,0:T(2,128)(2,1)S(1)} %bitcast.150, bf16[]{:T(256)} %broadcast.69), dimensions={1}, to_apply=%bitcast.90.reduce_sub_computation | reduce | bytes 1048578
  73.1 0.9 reshape.183
  74.1 4.3 all-to-all-done
  78.4 8.0 %all-to-all-start.2 = ((bf16[16,2,8192]{2,1,0:T(2,128)(2,1)}), bf16[16,2,8192]{2,1,0:T(2,128)(2,1)S(1)}, u32[]{:S(2)}, u32[]{:S(2)}) async-start(bf16[16,2,8192]{2,1,0:T(2,128)(2,1)} %reshape.183), calls=%async_computation.2 | async-start | bytes 1048576 | tf_op jit(solution)/shard_map/all_to_all | solution.py:28
  86.5 0.5 reshape.188
  87.5 0.5 reshape.186
  88.4 15.7 %all-to-all-done.2 = bf16[16,2,8192]{2,1,0:T(2,128)(2,1)S(1)} async-done(((bf16[16,2,8192]{2,1,0:T(2,128)(2,1)}), bf16[16,2,8192]{2,1,0:T(2,128)(2,1)S(1)}, u32[]{:S(2)}, u32[]{:S(2)}) %all-to-all-start.2) | async-done | bytes 524320 | tf_op jit(solution)/shard_map/all_to_all | solution.py:28
  104.1 0.9 stack.2
  105.0 9.1 %all-to-all-start.4 = ((bf16[32,128,64]{1,2,0:T(8,128)(2,1)}), bf16[32,128,64]{1,2,0:T(8,128)(2,1)S(1)}, u32[]{:S(2)}, u32[]{:S(2)}) async-start(bf16[32,128,64]{1,2,0:T(8,128)(2,1)} %stack.2), calls=%async_computation.4 | async-start | bytes 1048576 | tf_op jit(solution)/shard_map/all_to_all | solution.py:13
  114.1 0.5 reshape.184
  115.0 3.1 gather_fusion.1
  118.1 3.0 gather_fusion
  121.1 5.8 %fusion.58 = (f32[32,64]{1,0:T(8,128)S(1)}, f32[32,64,512]{2,1,0:T(8,128)}) fusion(bf16[32,512,128]{2,1,0:T(8,128)(2,1)} %bitcast.143, bf16[32,64,128]{2,1,0:T(8,128)(2,1)S(1)} %bitcast.170), kind=kOutput, calls=%fused_computation.49 | convolution fusion | flops 271581696 | bytes 8921088 | tf_op jit(solution)/shard_map/sub | solution.py:64
  126.9 4.3 convolution_convert_fusion
  131.3 8.1 %copy.136 = bf16[1,2048,128]{2,0,1:T(2,128)(2,1)S(1)} copy(bf16[1,2048,128]{2,1,0:T(8,128)(2,1)S(1)} %bitcast.152) | data formatting | bytes 1048576 | tf_op jit(solution)/shard_map/reshape;transpose;reshape | solution.py:45
  139.4 11.7 %reduce.9 = bf16[2048,128]{1,0:T(8,128)(2,1)S(1)} reduce(bf16[2048,1,128]{2,1,0:T(2,128)(2,1)S(1)} %bitcast.151, bf16[]{:T(256)} %broadcast.69), dimensions={1}, to_apply=%bitcast.127.reduce_sub_computation | reduce | bytes 1048578
  151.2 0.9 reshape.189
  152.1 8.2 %all-to-all-start.3 = ((bf16[16,2,8192]{2,1,0:T(2,128)(2,1)}), bf16[16,2,8192]{2,1,0:T(2,128)(2,1)S(1)}, u32[]{:S(2)}, u32[]{:S(2)}) async-start(bf16[16,2,8192]{2,1,0:T(2,128)(2,1)} %reshape.189), calls=%async_computation.3 | async-start | bytes 1048576 | tf_op jit(solution)/shard_map/all_to_all | solution.py:74
  160.3 80.0 %all-gather.2.cloned.1.call-done = bf16[1,2048,2048]{2,1,0:T(8,128)(2,1)} async-done(((bf16[1,128,2048]{2,1,0:T(8,128)(2,1)}), bf16[1,2048,2048]{2,1,0:T(8,128)(2,1)}) %all-gather.2.cloned.1.call-update) | async-done | bytes 8388624 | tf_op jit(solution)/shard_map/all_gather | solution.py:76
  240.2 5.9 %fusion.18 = bf16[2048,128]{1,0:T(8,128)(2,1)S(1)} fusion(bf16[128,2048]{0,1:T(8,128)(2,1)S(1)} %bitcast.172, bf16[1,2048,2048]{2,1,0:T(8,128)(2,1)} %all-gather.2.cloned.1.call-done), kind=kOutput, calls=%fused_computation.22 | convolution fusion | flops 1074003968 | bytes 9437184 | tf_op jit(solution)/shard_map/dot_general | solution.py:77
  246.1 3.5 fusion.61
  249.7 18.6 %fusion.42 = bf16[32,64,128]{2,1,0:T(8,128)(2,1)S(1)} fusion(bf16[32,512,128]{2,1,0:T(8,128)(2,1)} %bitcast.144, f32[32,64,512]{2,1,0:T(8,128)} %fusion.61, f32[32,64,512]{2,1,0:T(8,128)} %get-tuple-element.26, f32[32,64]{1,0:T(8,128)S(1)} %get-tuple-element.25), kind=kOutput, calls=%fused_computation.34 | convolution fusion | flops 276040192 | bytes 13115392 | tf_op jit(solution)/shard_map/hbqk,hbkd->hbqd/dot_general | solution.py:104
  268.2 8.1 %copy.135 = bf16[1,2048,128]{2,0,1:T(2,128)(2,1)S(1)} copy(bf16[1,2048,128]{2,1,0:T(8,128)(2,1)S(1)} %bitcast.169) | data formatting | bytes 1048576 | tf_op jit(solution)/shard_map/reshape;transpose;reshape | solution.py:45
  276.4 12.0 %reduce.10 = bf16[2048,128]{1,0:T(8,128)(2,1)S(1)} reduce(bf16[2048,1,128]{2,1,0:T(2,128)(2,1)S(1)} %bitcast.147, bf16[]{:T(256)} %broadcast.69), dimensions={1}, to_apply=%bitcast.126.reduce_sub_computation | reduce | bytes 1048578
  288.4 0.9 reshape.191
  289.3 7.2 %all-to-all-start.5 = ((bf16[16,2,8192]{2,1,0:T(2,128)(2,1)}), bf16[16,2,8192]{2,1,0:T(2,128)(2,1)S(1)}, u32[]{:S(2)}, u32[]{:S(2)}) async-start(bf16[16,2,8192]{2,1,0:T(2,128)(2,1)} %reshape.191), calls=%async_computation.5 | async-start | bytes 1048576 | tf_op jit(solution)/shard_map/all_to_all | solution.py:129
  296.6 7.8 %fusion.2 = f32[128,2048]{0,1:T(8,128)} fusion(bf16[2048,128]{1,0:T(8,128)(2,1)S(1)} %bitcast.153, bf16[1,2048,2048]{2,1,0:T(8,128)(2,1)} %all-gather.2.cloned.1.call-done), kind=kOutput, calls=%fused_computation.6 | convolution fusion | flops 1073741824 | bytes 9961472 | tf_op jit(solution)/shard_map/dot_general | solution.py:80
  304.4 20.8 %fusion.22 = f32[32,512,128]{2,1,0:T(8,128)} fusion(bf16[32,64,128]{2,1,0:T(8,128)(2,1)S(1)} %bitcast.171, f32[32,64,512]{2,1,0:T(8,128)} %fusion.61, f32[32,64,512]{2,1,0:T(8,128)} %get-tuple-element.26, f32[32,64]{1,0:T(8,128)S(1)} %get-tuple-element.25), kind=kOutput, calls=%fused_computation.23 | convolution fusion | flops 275778048 | bytes 17309696 | tf_op jit(solution)/shard_map/hbqk,hbqd->hbkd/dot_general | solution.py:107
  325.2 9.6 %reshape.150 = f32[32,8,8192]{2,1,0:T(8,128)} reshape(f32[32,512,128]{2,1,0:T(8,128)} %fusion.22) | data formatting | bytes 16777216 | tf_op jit(solution)/shard_map/reshape.36
  334.8 5.1 %copy.132 = f32[32,8,64,128]{3,2,1,0:T(8,128)S(1)} copy(f32[32,8,64,128]{3,1,2,0:T(8,128)} %bitcast.130) | data formatting | bytes 16777216
  339.9 8.2 %fusion.39 = bf16[32,64,128]{2,0,1:T(8,128)(2,1)S(1)} fusion(f32[64,128,32,8]{1,0,3,2:T(8,128)S(1)} %bitcast.131, s32[32,8]{0,1:T(8,128)S(1)} %bitcast.173), kind=kOutput, calls=%fused_computation.32 | convolution fusion | flops 805576704 | bytes 8913920 | tf_op jit(solution)/shard_map/hqsx,qsk->hkx/dot_general | solution.py:116
  348.3 8.3 %copy.134 = bf16[1,2048,128]{2,0,1:T(2,128)(2,1)S(1)} copy(bf16[1,2048,128]{2,1,0:T(8,128)(2,1)S(1)} %bitcast.157) | data formatting | bytes 1048576 | tf_op jit(solution)/shard_map/reshape;transpose;reshape | solution.py:45
  356.6 11.5 %reduce.11 = bf16[2048,128]{1,0:T(8,128)(2,1)S(1)} reduce(bf16[2048,1,128]{2,1,0:T(2,128)(2,1)S(1)} %bitcast.148, bf16[]{:T(256)} %broadcast.69), dimensions={1}, to_apply=%bitcast.125.reduce_sub_computation | reduce | bytes 1048578
  368.2 0.9 reshape.193
  369.1 8.6 %all-to-all-start.6 = ((bf16[16,2,8192]{2,1,0:T(2,128)(2,1)}), bf16[16,2,8192]{2,1,0:T(2,128)(2,1)S(1)}, u32[]{:S(2)}, u32[]{:S(2)}) async-start(bf16[16,2,8192]{2,1,0:T(2,128)(2,1)} %reshape.193), calls=%async_computation.6 | async-start | bytes 1048576 | tf_op jit(solution)/shard_map/all_to_all | solution.py:130
  377.7 7.2 %fusion.45 = f32[32,512,128]{2,1,0:T(8,128)} fusion(bf16[32,64,128]{2,1,0:T(8,128)(2,1)S(1)} %bitcast.168, f32[32,64,512]{2,1,0:T(8,128)} %get-tuple-element.26, f32[32,64]{1,0:T(8,128)S(1)} %get-tuple-element.25), kind=kOutput, calls=%fused_computation.35 | convolution fusion | flops 270532608 | bytes 13115392 | tf_op jit(solution)/shard_map/hbqk,hbqd->hbkd/dot_general | solution.py:88
  384.9 9.4 %reshape.151 = f32[32,8,8192]{2,1,0:T(8,128)} reshape(f32[32,512,128]{2,1,0:T(8,128)} %fusion.45) | data formatting | bytes 16777216 | tf_op jit(solution)/shard_map/reshape.43
  394.3 5.0 %copy.131 = f32[32,8,64,128]{3,2,1,0:T(8,128)S(1)} copy(f32[32,8,64,128]{3,1,2,0:T(8,128)} %bitcast.132) | data formatting | bytes 16777216
  399.3 8.2 %fusion.36 = bf16[32,64,128]{2,0,1:T(8,128)(2,1)S(1)} fusion(f32[64,128,32,8]{1,0,3,2:T(8,128)S(1)} %bitcast.133, s32[32,8]{0,1:T(8,128)S(1)} %bitcast.174), kind=kOutput, calls=%fused_computation.31 | convolution fusion | flops 805576704 | bytes 8913920 | tf_op jit(solution)/shard_map/hqsx,qsk->hkx/dot_general | solution.py:116
  407.7 8.3 %copy.133 = bf16[1,2048,128]{2,0,1:T(2,128)(2,1)S(1)} copy(bf16[1,2048,128]{2,1,0:T(8,128)(2,1)S(1)} %bitcast.158) | data formatting | bytes 1048576 | tf_op jit(solution)/shard_map/reshape;transpose;reshape | solution.py:45
  416.0 11.5 %reduce.12 = bf16[2048,128]{1,0:T(8,128)(2,1)S(1)} reduce(bf16[2048,1,128]{2,1,0:T(2,128)(2,1)S(1)} %bitcast.146, bf16[]{:T(256)} %broadcast.69), dimensions={1}, to_apply=%bitcast.124.reduce_sub_computation | reduce | bytes 1048578
  427.5 0.9 reshape.195
  428.5 8.1 %all-to-all-start.7 = ((bf16[16,2,8192]{2,1,0:T(2,128)(2,1)}), bf16[16,2,8192]{2,1,0:T(2,128)(2,1)S(1)}, u32[]{:S(2)}, u32[]{:S(2)}) async-start(bf16[16,2,8192]{2,1,0:T(2,128)(2,1)} %reshape.195), calls=%async_computation.7 | async-start | bytes 1048576 | tf_op jit(solution)/shard_map/all_to_all | solution.py:131
  436.6 0.5 reshape.190
  437.5 1.0 copy.98
  438.5 0.5 reshape.192
  439.4 1.0 copy.99
  440.4 0.5 reshape.194
  441.3 1.0 copy.100
  442.3 9.7 %all-to-all-done.7 = bf16[16,2,8192]{2,1,0:T(2,128)(2,1)S(1)} async-done(((bf16[16,2,8192]{2,1,0:T(2,128)(2,1)}), bf16[16,2,8192]{2,1,0:T(2,128)(2,1)S(1)}, u32[]{:S(2)}, u32[]{:S(2)}) %all-to-all-start.7) | async-done | bytes 524320 | tf_op jit(solution)/shard_map/all_to_all | solution.py:131
  452.0 0.5 reshape.196
  452.9 1.0 copy.101
  (42 shorter events, 3.2 us)
Async XLA Ops:
  7.2 27.9 %copy-start.1 = (bf16[1,128,2048]{2,1,0:T(8,128)(2,1)S(1)}, bf16[1,128,2048]{2,1,0:T(8,128)(2,1)}, u32[]{:S(2)}) copy-start(bf16[1,128,2048]{2,1,0:T(8,128)(2,1)} %param.7) | copy-start | bytes 1572868
  7.2 233.1 %all-gather.2.cloned.1.call-start = ((), (), s32[]{:S(2)}) async-start(), calls=%async_computation.9 | async-start | bytes 8912896 | tf_op jit(solution)/shard_map/all_gather | solution.py:76
  10.8 50.1 %copy-start.2 = (bf16[1,128,2048]{2,1,0:T(8,128)(2,1)S(1)}, bf16[1,128,2048]{2,1,0:T(8,128)(2,1)}, u32[]{:S(2)}) copy-start(bf16[1,128,2048]{2,1,0:T(8,128)(2,1)} %param.8) | copy-start | bytes 1572868
  23.3 27.8 %all-to-all-start.1 = ((bf16[16,2,8192]{2,1,0:T(2,128)(2,1)}), bf16[16,2,8192]{2,1,0:T(2,128)(2,1)S(1)}, u32[]{:S(2)}, u32[]{:S(2)}) async-start(bf16[16,2,8192]{2,1,0:T(2,128)(2,1)} %reshape.187), calls=%async_computation.1 | async-start | bytes 1048576 | tf_op jit(solution)/shard_map/all_to_all | solution.py:26
  35.8 50.5 %copy-start.5 = (s32[1,32,8]{1,2,0:T(8,128)S(1)}, s32[1,32,8]{1,2,0:T(8,128)}, u32[]{:S(2)}) copy-start(s32[1,32,8]{1,2,0:T(8,128)} %param.11) | copy-start | bytes 3076
  51.1 27.2 %all-to-all-start = ((bf16[16,2,8192]{2,1,0:T(2,128)(2,1)}), bf16[16,2,8192]{2,1,0:T(2,128)(2,1)S(1)}, u32[]{:S(2)}, u32[]{:S(2)}) async-start(bf16[16,2,8192]{2,1,0:T(2,128)(2,1)} %reshape.185), calls=%async_computation | async-start | bytes 1048576 | tf_op jit(solution)/shard_map/all_to_all | solution.py:27
  78.4 25.7 %all-to-all-start.2 = ((bf16[16,2,8192]{2,1,0:T(2,128)(2,1)}), bf16[16,2,8192]{2,1,0:T(2,128)(2,1)S(1)}, u32[]{:S(2)}, u32[]{:S(2)}) async-start(bf16[16,2,8192]{2,1,0:T(2,128)(2,1)} %reshape.183), calls=%async_computation.2 | async-start | bytes 1048576 | tf_op jit(solution)/shard_map/all_to_all | solution.py:28
  86.5 17.5 %copy-start.6 = (bf16[128,64]{0,1:T(8,128)(2,1)S(1)}, bf16[128,64]{0,1:T(8,128)(2,1)}, u32[]{:S(2)}) copy-start(bf16[128,64]{0,1:T(8,128)(2,1)} %param.9) | copy-start | bytes 49156
  87.4 33.7 %copy-start.3 = (bf16[1,16,128,128]{3,2,1,0:T(8,128)(2,1)}, bf16[1,16,128,128]{3,2,1,0:T(8,128)(2,1)S(1)}, u32[]{:S(2)}) copy-start(bf16[1,16,128,128]{3,2,1,0:T(8,128)(2,1)S(1)} %copy.83) | copy-start | bytes 1572868
  105.0 47.1 %all-to-all-start.4 = ((bf16[32,128,64]{1,2,0:T(8,128)(2,1)}), bf16[32,128,64]{1,2,0:T(8,128)(2,1)S(1)}, u32[]{:S(2)}, u32[]{:S(2)}) async-start(bf16[32,128,64]{1,2,0:T(8,128)(2,1)} %stack.2), calls=%async_computation.4 | async-start | bytes 1048576 | tf_op jit(solution)/shard_map/all_to_all | solution.py:13
  152.1 137.2 %all-to-all-start.3 = ((bf16[16,2,8192]{2,1,0:T(2,128)(2,1)}), bf16[16,2,8192]{2,1,0:T(2,128)(2,1)S(1)}, u32[]{:S(2)}, u32[]{:S(2)}) async-start(bf16[16,2,8192]{2,1,0:T(2,128)(2,1)} %reshape.189), calls=%async_computation.3 | async-start | bytes 1048576 | tf_op jit(solution)/shard_map/all_to_all | solution.py:74
  240.2 5.9 %copy-start = (bf16[256,64,128]{2,1,0:T(8,128)(2,1)S(1)}, bf16[256,64,128]{2,1,0:T(8,128)(2,1)}, u32[]{:S(2)}) copy-start(bf16[256,64,128]{2,1,0:T(8,128)(2,1)} %gather_fusion.1) | copy-start | bytes 12582916
  289.3 79.8 %all-to-all-start.5 = ((bf16[16,2,8192]{2,1,0:T(2,128)(2,1)}), bf16[16,2,8192]{2,1,0:T(2,128)(2,1)S(1)}, u32[]{:S(2)}, u32[]{:S(2)}) async-start(bf16[16,2,8192]{2,1,0:T(2,128)(2,1)} %reshape.191), calls=%async_computation.5 | async-start | bytes 1048576 | tf_op jit(solution)/shard_map/all_to_all | solution.py:129
  296.5 157.4 %reduce-scatter.2.cloned.1.call-start = ((), (), s32[]{:S(2)}) async-start(), calls=%async_computation.10 | async-start | bytes 1081344 | tf_op jit(solution)/shard_map/reduce_scatter | solution.py:21
  296.6 7.8 %copy-start.4 = (bf16[1,16,128,128]{3,2,1,0:T(8,128)(2,1)S(1)}, bf16[1,16,128,128]{3,2,1,0:T(8,128)(2,1)}, u32[]{:S(2)}) copy-start(bf16[1,16,128,128]{3,2,1,0:T(8,128)(2,1)} %copy-done.3) | copy-start | bytes 1572868
  369.1 59.4 %all-to-all-start.6 = ((bf16[16,2,8192]{2,1,0:T(2,128)(2,1)}), bf16[16,2,8192]{2,1,0:T(2,128)(2,1)S(1)}, u32[]{:S(2)}, u32[]{:S(2)}) async-start(bf16[16,2,8192]{2,1,0:T(2,128)(2,1)} %reshape.193), calls=%async_computation.6 | async-start | bytes 1048576 | tf_op jit(solution)/shard_map/all_to_all | solution.py:130
  428.5 23.6 %all-to-all-start.7 = ((bf16[16,2,8192]{2,1,0:T(2,128)(2,1)}), bf16[16,2,8192]{2,1,0:T(2,128)(2,1)S(1)}, u32[]{:S(2)}, u32[]{:S(2)}) async-start(bf16[16,2,8192]{2,1,0:T(2,128)(2,1)} %reshape.195), calls=%async_computation.7 | async-start | bytes 1048576 | tf_op jit(solution)/shard_map/all_to_all | solution.py:131
Sparse Core Ops, SparseCore 0:
  10.1 230.1 all-gather.1
  304.5 93.6 reduce-scatter.1
